TPU v7x, 512 devices: a whole 4x4x16 slice. The times are simulated.
512 devices in a mesh: val: 4 (over z_lo), cond: 16 (over y, z_hi), gcol: 8 (over x, core).
Axes of the slice: x: 4, y: 4, z: 16 (z_hi: 4, z_lo: 4; z = z_hi * 4 + z_lo), core: 2. Of those that a mesh axis runs over, the one named last changes fastest.
Arguments:
- psi_val: bfloat16 [2, 16, 72, 5184], P(None, 'val', 'gcol'), may hold values from -6 to 6
- psi_cond: bfloat16 [2, 32, 72, 5184], P(None, 'cond', 'gcol'), may hold values from -6 to 6
- energy_val: float32 [16], P('val'), may hold values from -12 to -2
- energy_cond: float32 [32], P('cond'), may hold values from 0.5 to 8
- occupancy: int32 [16], P('val'), may hold values from 1 to 2
- gmap: int32 [3, 5120], replicated, may hold values from 0 to 71, as said below
Outputs:
- chi: float32 [2, 5120, 5120], P(None, ('val', 'cond'), 'gcol')
Inputs may be any that keep to these rules, and one draw needn't show every extreme that they name: `gmap`: the 5120 columns are distinct grid frequencies: the 5120 of smallest kx^2 + ky^2 + kz^2 when each coordinate k is read as k - 72 where it exceeds 72 / 2 (ties at the outermost radius taken in any way), in any order.
All inputs are finite; a program needn't handle non-finite values.
Results may differ from a plain program's by a relative error of at most 0.0039.
Values may be sent and summed in bfloat16 or wider, within the bound.
A program may use at most 128 MiB of HBM per device.

v0:
```python
import math

import jax
import jax.numpy as jnp
from jax import lax
from jax.sharding import PartitionSpec as P

NX = 72
NY = 72
NZ = 72
NG = 5120


def fourier_table(length):
    counter = jnp.arange(length, dtype=jnp.int32)
    products = counter[:, None] * counter[None, :] % length
    angles = products.astype(jnp.float32) * (2.0 * math.pi / length)
    normal_scale = 1.0 / math.sqrt(length)
    cosine_table = jnp.cos(angles) * normal_scale
    sine_table = jnp.sin(angles) * normal_scale
    return jnp.stack(
        [
            jnp.stack([cosine_table, -sine_table], axis=1),
            jnp.stack([sine_table, cosine_table], axis=1),
        ],
        axis=0,
    )


def depth_phases(depth_size, positions, freq_z):
    products = freq_z[:, None] * positions[None, :] % depth_size
    angles = products.astype(jnp.float32) * (2.0 * math.pi / depth_size)
    normal_scale = 1.0 / math.sqrt(depth_size)
    return (jnp.cos(angles) * normal_scale, jnp.sin(angles) * normal_scale)


def pair_product(valence, conduction):
    real_val = valence[0][:, None]
    imag_val = valence[1][:, None]
    real_cond = conduction[0][None]
    imag_cond = conduction[1][None]
    return jnp.stack(
        [real_val * real_cond + imag_val * imag_cond, real_val * imag_cond - imag_val * real_cond]
    )


def plane_transform(pair_field, table_x, table_y):
    first_pass = jnp.einsum("rbxy,rxsk->skyb", pair_field, table_x, precision=lax.Precision.HIGHEST)
    return jnp.einsum("skyb,sytl->tklb", first_pass, table_y, precision=lax.Precision.HIGHEST)


def select_planes(plane_field, grid_rows, cosine_table, sine_table):
    picked = plane_field[:, grid_rows]
    high = lax.Precision.HIGHEST
    real_part = jnp.einsum("gpz,gz->pg", picked[0], cosine_table, precision=high) + jnp.einsum(
        "gpz,gz->pg", picked[1], sine_table, precision=high
    )
    imag_part = jnp.einsum("gpz,gz->pg", picked[1], cosine_table, precision=high) - jnp.einsum(
        "gpz,gz->pg", picked[0], sine_table, precision=high
    )
    return jnp.stack([real_part, imag_part])


def add_products(row_side, incoming):
    real_part = jnp.einsum("spr,spc->rc", row_side, incoming, preferred_element_type=jnp.float32)
    imag_part = jnp.einsum(
        "pr,pc->rc", row_side[1], incoming[0], preferred_element_type=jnp.float32
    ) - jnp.einsum("pr,pc->rc", row_side[0], incoming[1], preferred_element_type=jnp.float32)
    return jnp.stack([real_part, imag_part])


def shards(psi_val, psi_cond, energy_val, energy_cond, occupancy, gmap):
    groups = lax.axis_size("gcol")
    band_count = psi_val.shape[1]
    depth_local = psi_val.shape[2]
    cond_bands = psi_cond.shape[1]
    band_block = 4
    block_count = band_count // band_block
    column_width = NG // groups
    table_x = fourier_table(NX)
    table_y = fourier_table(NY)
    grid_rows = gmap[0] * NY + gmap[1]
    positions = lax.axis_index("gcol") * depth_local + jnp.arange(depth_local, dtype=jnp.int32)
    cosine_table, sine_table = depth_phases(NZ, positions, gmap[2])
    row_groups = grid_rows.reshape(groups, column_width)
    cosine_groups = cosine_table.reshape(groups, column_width, depth_local)
    sine_groups = sine_table.reshape(groups, column_width, depth_local)
    conduction = psi_cond.astype(jnp.float32)

    def block_elements(valence):
        pair_field = pair_product(valence.astype(jnp.float32), conduction)
        pair_field = pair_field.reshape(2, band_block * cond_bands * depth_local, NX, NY)
        plane_field = plane_transform(pair_field, table_x, table_y).reshape(
            2, NX * NY, band_block * cond_bands, depth_local
        )

        def slice_elements(operands):
            index_rows, cosine_part, sine_part = operands
            return select_planes(plane_field, index_rows, cosine_part, sine_part)

        pieces = lax.map(slice_elements, (row_groups, cosine_groups, sine_groups))
        return jnp.moveaxis(pieces, 0, 2).reshape(2, band_block * cond_bands, NG)

    valence_blocks = jnp.moveaxis(
        psi_val.reshape(2, block_count, band_block, depth_local, NX * NY), 1, 0
    )
    blocks = lax.map(block_elements, valence_blocks)
    partial_sums = jnp.moveaxis(blocks, 0, 1).reshape(2, band_count * cond_bands, NG)
    factor = (
        occupancy.astype(jnp.float32)[:, None] / (energy_cond[None, :] - energy_val[:, None])
    ).reshape(band_count * cond_bands)
    elements = lax.psum(partial_sums, "gcol")
    plain_elements = elements.astype(jnp.bfloat16)
    weighted = (elements * factor[None, :, None]).astype(jnp.bfloat16)
    column_side = lax.dynamic_slice_in_dim(
        weighted, lax.axis_index("gcol") * column_width, column_width, 2
    )
    val_count = lax.axis_size("val")
    cond_count = lax.axis_size("cond")
    pair_count = band_count * cond_bands
    row_width = NG // (val_count * cond_count)
    pair_scale = 1.0 / math.sqrt(pair_count * val_count * cond_count)
    outgoing = plain_elements.reshape(2, pair_count, val_count * cond_count, row_width)
    row_side = lax.all_to_all(
        outgoing, ("val", "cond"), split_axis=2, concat_axis=1, tiled=True
    ).reshape(2, pair_count * val_count * cond_count, row_width)
    chi_tile = add_products(
        row_side, lax.all_gather(column_side, ("val", "cond"), axis=1, tiled=True)
    )
    return chi_tile * pair_scale


def solution(mesh):
    return jax.shard_map(
        shards,
        mesh=mesh,
        in_specs=(
            P(None, "val", "gcol", None),
            P(None, "cond", "gcol", None),
            P("val"),
            P("cond"),
            P("val"),
            P(),
        ),
        out_specs=P(None, ("val", "cond"), "gcol"),
        check_vma=False,
    )
```

profile of v0, /device:TPU:38, one launch (start us, length us, event | category | flops | bytes accessed | tf_op | source)
XLA Modules:
  0.0 686.4 jit_solution(11545037893729943024)
XLA Ops:
  6.9 1.2 convert_element_type.48
  8.5 0.7 copy-done.2
  9.2 0.3 convert_element_type.49
  9.7 2.1 multiply_add_fusion
  11.8 4.1 add.103
  15.9 3.3 copy.28
  19.1 2.8 sub.44
  21.9 3.4 copy.29
  25.3 8.7 %fusion.5 = f32[2,72,72,72,1]{1,2,0,3,4:T(8,128)} fusion(f32[1,72,72,72]{2,3,0,1:T(8,128)} %copy.29, f32[1,72,72,72]{2,3,0,1:T(8,128)S(1)} %copy-done, f32[1,72,2,72]{3,1,0,2:T(8,128)S(1)} %get-tuple-element.124, f32[1,72,2,72]{3,1,0,2:T(8,128)S(1)} %get-tuple-element.123), kind=kOutput, calls=%fused_computation.22 | convolution fusion | flops 1290712320 | bytes 6054912 | tf_op jit(solution)/shard_map/while/body/eval_jaxpr/rbxy,rxsk->skyb/dot_general | solution.py:48
  34.1 6.2 copy.60
  40.3 9.4 %convolution_bitcast_fusion = f32[2,72,72,72]{2,3,0,1:T(8,128)} fusion(f32[2,72,72,72,1]{2,3,0,4,1:T(8,128)} %copy.60, f32[1,72,2,72]{3,1,0,2:T(8,128)S(1)} %get-tuple-element.124, f32[1,72,2,72]{3,1,0,2:T(8,128)S(1)} %get-tuple-element.123), kind=kOutput, calls=%fused_computation.23 | convolution fusion | flops 1289965824 | bytes 6054912 | tf_op jit(solution)/shard_map/while/body/eval_jaxpr/skyb,sytl->tklb/dot_general | solution.py:49
  49.6 6.0 copy.65
  55.6 24.3 %reshape.308 = f32[2,5184,8,9]{3,2,1,0:T(8,128)} reshape(f32[2,72,72,72]{3,2,1,0:T(8,128)} %copy.65) | data formatting | bytes 5971968 | tf_op jit(solution)/shard_map/while/body/eval_jaxpr/while | solution.py:101
  80.1 1.4 sine_multiply_fusion
  81.6 128.6 %while.21 = (s32[]{:T(128)}, f32[8,2,8,640]{3,2,1,0:T(8,128)S(1)}, f32[8,640,9]{1,2,0:T(8,128)S(1)}, s32[8,640]{1,0:T(8,128)S(1)}, f32[2,5184,8,9]{3,2,1,0:T(8,128)}, /*index=5*/f32[8,640,9]{1,2,0:T(8,128)S(1)}, s32[]{:T(128)}) while((s32[]{:T(128)}, f32[8,2,8,640]{3,2,1,0:T(8,128)S(1)}, f32[8,640,9]{1,2,0:T(8,128)S(1)}, ...), condition=%wide.region_1.2_spmd, body=%wide.region_0.1_spmd.sunk | while | flops 371586 | bytes 1801305 | solution.py:101
  81.8 0.2 copy.80
  82.0 9.7 %gather_fusion = f32[640,2,8,9]{3,2,1,0:T(8,128)} fusion(f32[2,5184,8,9]{3,2,1,0:T(8,128)} %get-tuple-element.196, s32[1024]{0:T(1024)S(1)} %pad_clamp_fusion.2), kind=kCustom, calls=%fused_computation.clone.1 | custom fusion | bytes 739840 | tf_op jit(solution)/shard_map/while/body/eval_jaxpr/while/body/eval_jaxpr/gather | solution.py:53
  91.7 5.4 multiply_reduce_fusion.5
  98.1 9.7 %gather_fusion = f32[640,2,8,9]{3,2,1,0:T(8,128)} fusion(f32[2,5184,8,9]{3,2,1,0:T(8,128)} %get-tuple-element.196, s32[1024]{0:T(1024)S(1)} %pad_clamp_fusion.2), kind=kCustom, calls=%fused_computation.clone.1 | custom fusion | bytes 739840 | tf_op jit(solution)/shard_map/while/body/eval_jaxpr/while/body/eval_jaxpr/gather | solution.py:53
  107.7 5.4 multiply_reduce_fusion.5
  113.9 0.2 copy.80
  114.1 9.7 %gather_fusion = f32[640,2,8,9]{3,2,1,0:T(8,128)} fusion(f32[2,5184,8,9]{3,2,1,0:T(8,128)} %get-tuple-element.196, s32[1024]{0:T(1024)S(1)} %pad_clamp_fusion.2), kind=kCustom, calls=%fused_computation.clone.1 | custom fusion | bytes 739840 | tf_op jit(solution)/shard_map/while/body/eval_jaxpr/while/body/eval_jaxpr/gather | solution.py:53
  123.8 5.4 multiply_reduce_fusion.5
  130.2 9.7 %gather_fusion = f32[640,2,8,9]{3,2,1,0:T(8,128)} fusion(f32[2,5184,8,9]{3,2,1,0:T(8,128)} %get-tuple-element.196, s32[1024]{0:T(1024)S(1)} %pad_clamp_fusion.2), kind=kCustom, calls=%fused_computation.clone.1 | custom fusion | bytes 739840 | tf_op jit(solution)/shard_map/while/body/eval_jaxpr/while/body/eval_jaxpr/gather | solution.py:53
  139.9 5.4 multiply_reduce_fusion.5
  146.0 0.2 copy.80
  146.3 9.7 %gather_fusion = f32[640,2,8,9]{3,2,1,0:T(8,128)} fusion(f32[2,5184,8,9]{3,2,1,0:T(8,128)} %get-tuple-element.196, s32[1024]{0:T(1024)S(1)} %pad_clamp_fusion.2), kind=kCustom, calls=%fused_computation.clone.1 | custom fusion | bytes 739840 | tf_op jit(solution)/shard_map/while/body/eval_jaxpr/while/body/eval_jaxpr/gather | solution.py:53
  156.0 5.4 multiply_reduce_fusion.5
  162.3 9.7 %gather_fusion = f32[640,2,8,9]{3,2,1,0:T(8,128)} fusion(f32[2,5184,8,9]{3,2,1,0:T(8,128)} %get-tuple-element.196, s32[1024]{0:T(1024)S(1)} %pad_clamp_fusion.2), kind=kCustom, calls=%fused_computation.clone.1 | custom fusion | bytes 739840 | tf_op jit(solution)/shard_map/while/body/eval_jaxpr/while/body/eval_jaxpr/gather | solution.py:53
  172.0 5.4 multiply_reduce_fusion.5
  178.2 0.2 copy.80
  178.4 9.7 %gather_fusion = f32[640,2,8,9]{3,2,1,0:T(8,128)} fusion(f32[2,5184,8,9]{3,2,1,0:T(8,128)} %get-tuple-element.196, s32[1024]{0:T(1024)S(1)} %pad_clamp_fusion.2), kind=kCustom, calls=%fused_computation.clone.1 | custom fusion | bytes 739840 | tf_op jit(solution)/shard_map/while/body/eval_jaxpr/while/body/eval_jaxpr/gather | solution.py:53
  188.1 5.4 multiply_reduce_fusion.5
  194.3 0.2 copy.80
  194.5 9.7 %gather_fusion = f32[640,2,8,9]{3,2,1,0:T(8,128)} fusion(f32[2,5184,8,9]{3,2,1,0:T(8,128)} %get-tuple-element.196, s32[1024]{0:T(1024)S(1)} %pad_clamp_fusion.2), kind=kCustom, calls=%fused_computation.clone.1 | custom fusion | bytes 739840 | tf_op jit(solution)/shard_map/while/body/eval_jaxpr/while/body/eval_jaxpr/gather | solution.py:53
  204.2 5.4 multiply_reduce_fusion.5
  210.2 0.7 copy.34
  211.2 77.3 %all-reduce.2.cloned.1.call-done = f32[2,8,5120]{2,1,0:T(8,128)} async-done(((f32[2,8,5120]{2,1,0:T(8,128)}), f32[2,8,5120]{2,1,0:T(8,128)}) %all-reduce.2.cloned.1.call-update) | async-done | bytes 327696 | tf_op jit(solution)/shard_map/psum | solution.py:112
  288.5 1.5 fusion.15
  290.0 1.0 convert_element_type.51
  291.0 0.3 reshape.284
  291.3 0.2 copy.35
  291.5 41.3 %all_to_all.15 = bf16[2,8,64,80]{3,1,0,2:T(8,128)(2,1)S(1)} all-to-all(bf16[2,8,64,80]{3,1,0,2:T(8,128)(2,1)S(1)} %copy.35), channel_id=1, replica_groups=mesh['val'=4,'cond'=16,'gcol'=8] {'val','cond'}, dimensions={2} | all-to-all | bytes 327680 | tf_op jit(solution)/shard_map/all_to_all | solution.py:124
  332.7 342.6 %all-gather.2.cloned.1.call-done = bf16[2,512,640]{2,1,0:T(8,128)(2,1)} async-done(((bf16[2,8,640]{2,1,0:T(8,128)(2,1)}), bf16[2,512,640]{2,1,0:T(8,128)(2,1)}) %all-gather.2.cloned.1.call-update) | async-done | bytes 1310736 | tf_op jit(solution)/shard_map/all_gather | solution.py:128
  675.4 1.8 convolution_bitcast_fusion.1
  677.2 1.3 fusion.7
  678.5 0.3 fusion.6
  678.8 0.8 maximum_multiply_fusion
  (125 shorter events, 7.9 us)
Async XLA Ops:
  6.5 281.9 %all-reduce.2.cloned.1.call-start = ((), (), s32[]{:S(2)}) async-start(), calls=%async_computation.1 | async-start | bytes 655360 | tf_op jit(solution)/shard_map/psum | solution.py:112
  8.2 1.0 copy-start.2
  21.9 3.4 copy-start
  55.6 24.3 %copy-start.3 = (s32[3,5120]{1,0:T(4,128)S(1)}, s32[3,5120]{1,0:T(4,128)}, u32[]{:S(2)}) copy-start(s32[3,5120]{1,0:T(4,128)} %param.13) | copy-start | bytes 184324
  81.5 129.5 %copy-start.6 = (s32[4]{0:T(128)S(1)}, s32[4]{0:T(128)}, u32[]{:S(2)}) copy-start(s32[4]{0:T(128)} %param.12) | copy-start | bytes 52
  81.5 129.5 %copy-start.4 = (f32[4]{0:T(128)S(1)}, f32[4]{0:T(128)}, u32[]{:S(2)}) copy-start(f32[4]{0:T(128)} %param.10) | copy-start | bytes 52
  81.5 129.5 %copy-start.5 = (f32[2]{0:T(128)S(1)}, f32[2]{0:T(128)}, u32[]{:S(2)}) copy-start(f32[2]{0:T(128)} %param.11) | copy-start | bytes 28
  210.9 464.5 %all-gather.2.cloned.1.call-start = ((), (), s32[]{:S(2)}) async-start(), calls=%async_computation.2 | async-start | bytes 1331200 | tf_op jit(solution)/shard_map/all_gather | solution.py:128
  675.4 3.1 copy-start.1
Sparse Core Ops, SparseCore 0:
  211.0 77.3 all-reduce.1
  290.8 384.5 all-gather.1
where the time goes:
time: 690 us; the launch traced here: 686 us
  waiting for transfers between devices  420 us (61%)
  local copies, waits for them, and re-layouts  137 us (20%)
  other arithmetic  52.4 us (8%)
  blocking collectives  41.3 us (6%)
  matrix products  21.5 us (3%)
  between operations  13.6 us (2%)
    all_gather x1, waiting for transfers between devices, shards(): lax.all_gather(column_side, ('val', 'cond'), axis=1, tiled=True)  343 us
    gather x8, local copies, waits for them, and re-layouts, select_planes(): picked = plane_field[:, grid_rows]  77.4 us
    psum x1, waiting for transfers between devices, shards(): elements = lax.psum(partial_sums, 'gcol')  77.3 us
    while x8, other arithmetic  43.1 us
    all_to_all x1, blocking collectives, shards(): lax.all_to_all(outgoing, ('val', 'cond'), split_axis=2, concat_axis=1, ti...  41.3 us
    while x2, local copies, waits for them, and re-layouts, block_elements(): pieces = lax.map(slice_elements, (row_groups, cosine_groups, sine_groups))  30.3 us
  transfers between devices with their start and end apart: 2, of which 2 were waited for; matrix products, arithmetic and copies ran while one was open for 0% of the time, Pallas kernels for 0%

commit v1 on v0

v1 whole, which is shorter than its diff:
```python
import math

import jax
import jax.numpy as jnp
import numpy as np
from jax import lax
from jax.experimental import pallas as pl
from jax.experimental.pallas import tpu as pltpu
from jax.sharding import PartitionSpec as P

MESH = pl.DeviceIdType.MESH
LENGTH = 72
NG = 5120
REACH = 10
SIDE = 2 * REACH + 1
HALF = (REACH + 1) * SIDE
CHUNK_X = 16
CHUNK = CHUNK_X * LENGTH
CHUNKS = 5
DEPTH = 9
WIDTH = 640
ROWS = 80
PLANES = 144
F32 = jnp.float32
BF16 = jnp.bfloat16


def split_bf16(table):
    high = table.astype(np.float32).astype(jnp.bfloat16)
    low = (table - high.astype(np.float64)).astype(np.float32).astype(jnp.bfloat16)
    return high, low


def plane_tables():
    point = np.arange(CHUNK)
    column = np.arange(HALF)
    kx, ky = column // SIDE, column % SIDE - REACH
    turns = (point[:, None] // LENGTH * kx[None] + point[:, None] % LENGTH * ky[None]) % LENGTH
    angles = turns * (2.0 * math.pi / LENGTH)
    table = np.zeros((CHUNK, 512))
    table[:, :HALF] = np.cos(angles) / LENGTH
    table[:, 256 : 256 + HALF] = np.sin(angles) / LENGTH
    high, low = split_bf16(table)
    turned = np.zeros((16, 256), np.float32)
    for chunk in range(CHUNKS):
        shift = (kx * CHUNK_X * chunk) % LENGTH * (2.0 * math.pi / LENGTH)
        turned[2 * chunk, :HALF] = np.cos(shift)
        turned[2 * chunk + 1, :HALF] = np.sin(shift)
    return np.stack([high, low]), turned


def depth_tables():
    kz = np.arange(SIDE) - REACH
    out = np.zeros((8, 64, 256), jnp.bfloat16)
    for group in range(8):
        z = group * DEPTH + np.arange(DEPTH)
        angles = (z[:, None] * kz[None]) % LENGTH * (2.0 * math.pi / LENGTH)
        rows = np.concatenate([np.cos(angles), np.sin(angles)]) / math.sqrt(LENGTH)
        high, low = split_bf16(rows)
        out[group, 0:18, HALF : HALF + SIDE] = high
        out[group, 32:50, HALF : HALF + SIDE] = low
    return out


def dot(a, b):
    return lax.dot_general(a, b, (((1,), (0,)), ((), ())), preferred_element_type=F32)


def kernel(
    val_hbm, cond_hbm, gmap_ref, ev_ref, ec_ref, occ_ref, table_hbm, turn_ref, depth_ref,
    out_ref,
    val_ref, cond_ref, table_ref, index_ref, high_ref, low_ref, left_ref, right_ref,
    part, sib, xout, xin, gathered, row_buf,
    in_sem, sib_s, sib_r, xs, xr, zs, zr, ys, yr, rs, rr,
):
    z_lo = lax.axis_index("val")
    cond = lax.axis_index("cond")
    gcol = lax.axis_index("gcol")
    y, z_hi = cond // 4, cond % 4
    z = z_hi * 4 + z_lo
    x, core = gcol // 2, gcol % 2

    def device(x_at, y_at, z_at, core_at):
        return (z_at % 4, y_at * 4 + z_at // 4, x_at * 2 + core_at)

    def z_peer(step):
        return device(x, y, (z + step + 16) % 16, core)

    def y_peer(step):
        return device(x, (y + step) % 4, z, core)

    def x_peer(step):
        return device((x + step) % 4, y, z, core)

    def g_peer(step):
        return (z_lo, cond, (gcol + step) % 8)

    def remote(src, dst, send, recv, target):
        return pltpu.make_async_remote_copy(
            src_ref=src, dst_ref=dst, send_sem=send, recv_sem=recv, device_id=target, device_id_type=MESH
        )

    peers = [g_peer(s) for s in range(1, 8)]
    peers += [z_peer(s) for s in (1, 2, 4, 8, 12, 14, 15)]
    peers += [y_peer(s) for s in (1, 2, 3)]
    barrier = pltpu.get_barrier_semaphore()
    for peer in peers:
        pl.semaphore_signal(barrier, inc=1, device_id=peer, device_id_type=MESH)

    loads = [
        pltpu.make_async_copy(val_hbm, val_ref, in_sem.at[0]),
        pltpu.make_async_copy(cond_hbm, cond_ref, in_sem.at[1]),
        pltpu.make_async_copy(table_hbm, table_ref, in_sem.at[2]),
    ]
    for load in loads:
        load.start()

    freq = gmap_ref[...]
    freq = jnp.where(freq > LENGTH // 2, freq - LENGTH, freq)
    kx, ky, kz = freq[0:1], freq[1:2], freq[2:3]
    flip = kx < 0
    index_ref[0:1, :] = jnp.where(flip, -kx, kx) * SIDE + jnp.where(flip, -ky, ky) + REACH
    index_ref[1:2, :] = jnp.where(flip, -1, 1)
    index_ref[2:3, :] = kz + (REACH + HALF)
    pad = (CHUNKS - 1) * PLANES
    high_ref[pad:, 576:] = jnp.zeros((PLANES, CHUNK - 576), BF16)
    low_ref[pad:, 576:] = jnp.zeros((PLANES, CHUNK - 576), BF16)
    loads[0].wait()
    loads[1].wait()

    for chunk in range(CHUNKS):
        for begin, width in ((0, 384), (384, 384), (768, 384)) if chunk < 4 else ((0, 384), (384, 192)):
            span = pl.ds(chunk * CHUNK + begin, width)
            v = [[val_ref[c, b, :, span].astype(F32) for b in range(4)] for c in range(2)]
            w = [[cond_ref[c, b, :, span].astype(F32) for b in range(2)] for c in range(2)]
            sub = lax.broadcasted_iota(jnp.int32, (8, width), 0)

            def last(rows, count):
                spread = [jnp.broadcast_to(r[8:9], (8, width)) for r in rows]
                if count == 2:
                    return jnp.where(sub % 2 == 0, spread[0], spread[1])
                lower = jnp.where(sub < 2, spread[0], spread[1])
                upper = jnp.where(sub < 6, spread[2], spread[3])
                return jnp.where(sub < 4, lower, upper)

            real, imag = [], []
            for b in range(4):
                for d in range(2):
                    vr, vi, wr, wi = v[0][b][0:8], v[1][b][0:8], w[0][d][0:8], w[1][d][0:8]
                    real.append(vr * wr + vi * wi)
                    imag.append(vr * wi - vi * wr)
            vr, vi, wr, wi = last(v[0], 4), last(v[1], 4), last(w[0], 2), last(w[1], 2)
            real.append(vr * wr + vi * wi)
            imag.append(vr * wi - vi * wr)
            field = jnp.concatenate(real + imag, axis=0)
            high = field.astype(BF16)
            low = (field - high.astype(F32)).astype(BF16)
            rows = slice(chunk * PLANES, (chunk + 1) * PLANES)
            high_ref[rows, begin : begin + width] = high
            low_ref[rows, begin : begin + width] = low

    loads[2].wait()
    planes = dot(high_ref[...], table_ref[0]) + dot(low_ref[...], table_ref[0]) + dot(high_ref[...], table_ref[1])
    cos_sum = planes[0:PLANES, 0:256]
    sin_sum = planes[0:PLANES, 256:512]
    for chunk in range(1, CHUNKS):
        at = chunk * PLANES
        c_part, s_part = planes[at : at + PLANES, 0:256], planes[at : at + PLANES, 256:512]
        c_turn, s_turn = turn_ref[2 * chunk : 2 * chunk + 1, :], turn_ref[2 * chunk + 1 : 2 * chunk + 2, :]
        cos_sum += c_turn * c_part - s_turn * s_part
        sin_sum += s_turn * c_part + c_turn * s_part

    def by_plane(rows):
        first = jnp.swapaxes(rows[0:64].reshape(8, 8, 256), 0, 1).reshape(64, 256)
        return jnp.concatenate([first, rows[64:72]], axis=0)

    even = jnp.concatenate([by_plane(cos_sum[0:72]), by_plane(cos_sum[72:144])], axis=0)
    odd = jnp.concatenate([by_plane(sin_sum[72:144]), -by_plane(sin_sum[0:72])], axis=0)
    even_high, odd_high = even.astype(BF16), odd.astype(BF16)
    left_ref[0:144, :] = even_high
    left_ref[144:288, :] = (even - even_high.astype(F32)).astype(BF16)
    left_ref[288:352, :] = depth_ref[gcol]
    right_ref[0:144, :] = odd_high
    right_ref[144:288, :] = (odd - odd_high.astype(F32)).astype(BF16)

    place = lax.broadcasted_iota(jnp.int32, (256, 256), 0)

    def block(step):
        target = (x + 3 - step) % 4
        for piece in range(5):
            span = pl.ds(pl.multiple_of(target * 1280 + piece * 256, 256), 256)
            hit = place == index_ref[0:1, span]
            phase = place == index_ref[2:3, span]
            pick = jnp.where(hit | phase, 1.0, 0.0).astype(BF16)
            signed = jnp.where(hit, index_ref[1:2, span].astype(F32), 0.0).astype(BF16)
            first = dot(left_ref[...], pick)
            second = dot(right_ref[...], signed)
            values = first[0:144] + first[144:288] + second[0:144] + second[144:288]
            phases = first[288:306] + first[320:338]
            real, imag = None, None
            for d in range(DEPTH):
                re, im = values[8 * d : 8 * d + 8], values[72 + 8 * d : 80 + 8 * d]
                c, s = phases[d : d + 1], phases[DEPTH + d : DEPTH + d + 1]
                r_term, i_term = re * c + im * s, im * c - re * s
                real = r_term if real is None else real + r_term
                imag = i_term if imag is None else imag + i_term
            both = jnp.concatenate([real, imag], axis=0)
            for q in range(2):
                at = piece * 256 + q * 128
                part[step, at // WIDTH, :, at % WIDTH : at % WIDTH + 128] = both[:, q * 128 : (q + 1) * 128]

    sib_copies = [
        remote(part.at[j, 1 - core], sib.at[j], sib_s.at[j], sib_r.at[j], device(x, y, z, 1 - core)) for j in range(4)
    ]
    x_copies = [remote(xout.at[j], xin.at[j], xs.at[j], xr.at[j], x_peer(3 - j)) for j in range(3)]
    for j in range(4):
        block(j)
        if j == 0:
            pl.semaphore_wait(barrier, len(peers))
        sib_copies[j].start()
        if j > 0:
            sib_copies[j - 1].wait_recv()
            xout[j - 1] = part[j - 1, core] + sib[j - 1]
            x_copies[j - 1].start()

    pair = lax.broadcasted_iota(jnp.int32, (16, 1), 0) % 8
    e_val = jnp.zeros((16, 1), F32)
    e_cond = jnp.zeros((16, 1), F32)
    occupied = jnp.zeros((16, 1), F32)
    for b in range(4):
        e_val = jnp.where(pair // 2 == b, ev_ref[b], e_val)
        occupied = jnp.where(pair // 2 == b, occ_ref[b].astype(F32), occupied)
    for d in range(2):
        e_cond = jnp.where(pair % 2 == d, ec_ref[d], e_cond)
    factor = jnp.sqrt(occupied / (e_cond - e_val) * (1.0 / math.sqrt(512.0)))

    sib_copies[3].wait_recv()
    total = part[3, core] + sib[3]
    for j in range(3):
        x_copies[j].wait_recv()
        total += xin[j]
    gathered[0, 0] = (total * factor).astype(BF16)

    z_copies = [
        remote(gathered.at[0, 0], gathered.at[0, a], zs.at[a], zr.at[a], z_peer(4 * a)) for a in (2, 1, 3)
    ]
    for copy in z_copies:
        copy.start()
    for copy in z_copies:
        copy.wait_recv()
    near = [(1, 0, 4, 4), (15, 0, 12, 4), (2, 1, 8, 2), (14, 0, 10, 2)]
    near_copies = [
        remote(gathered.at[0, pl.ds(src, n)], gathered.at[0, pl.ds(dst, n)], zs.at[4 + i], zr.at[4 + i], z_peer(step))
        for i, (step, src, dst, n) in enumerate(near)
    ]
    for copy in near_copies:
        copy.start()
    for copy in near_copies:
        copy.wait_recv()
    y_copies = {j: remote(gathered.at[0], gathered.at[j], ys.at[j], yr.at[j], y_peer(j)) for j in (1, 3, 2)}
    for j in (1, 3, 2):
        y_copies[j].start()

    is_source = gcol == z_lo * 2 + cond // 8
    offset = cond % 8 * ROWS
    chosen = jnp.where(
        lax.broadcasted_iota(jnp.int32, (ROWS, WIDTH), 1)
        == lax.broadcasted_iota(jnp.int32, (ROWS, WIDTH), 0) + offset,
        1.0,
        0.0,
    ).astype(BF16)
    k_row = lax.broadcasted_iota(jnp.int32, (256, 256), 0)
    k_col = lax.broadcasted_iota(jnp.int32, (256, 256), 1)
    is_real = k_col // 8 % 2 == 0
    turn_i = jnp.where(
        is_real & (k_row == k_col + 8), 1.0, jnp.where(~is_real & (k_row == k_col - 8), -1.0, 0.0)
    ).astype(BF16)

    def row_copy(j, step):
        return remote(row_buf.at[j], row_buf.at[j], rs.at[j, step], rr.at[j], g_peer(step))

    def share_rows(j):
        @pl.when(is_source)
        def _():
            columns = gathered[j].reshape(256, WIDTH)
            rows = lax.dot_general(chosen, columns, (((1,), (1,)), ((), ())), preferred_element_type=F32)
            row_buf[j] = rows.astype(BF16)
            for step in range(1, 8):
                row_copy(j, step).start()

    def use(j, first):
        @pl.when(jnp.logical_not(is_source))
        def _():
            row_copy(j, 1).wait_recv()

        rows = row_buf[j]
        rows_i = dot(rows, turn_i).astype(BF16)
        columns = gathered[j].reshape(256, WIDTH)
        real, imag = dot(rows, columns), dot(rows_i, columns)
        if first:
            out_ref[0] = real
            out_ref[1] = imag
        else:
            out_ref[0] += real
            out_ref[1] += imag

    share_rows(0)
    y_copies[1].wait_recv()
    share_rows(1)
    use(0, True)
    y_copies[3].wait_recv()
    share_rows(3)
    use(1, False)
    y_copies[2].wait_recv()
    share_rows(2)
    use(3, False)
    use(2, False)

    @pl.when(is_source)
    def _():
        for j in range(4):
            for step in range(1, 8):
                row_copy(j, step).wait_send()

    for copy in sib_copies + x_copies + z_copies + near_copies + list(y_copies.values()):
        copy.wait_send()


def shards(psi_val, psi_cond, energy_val, energy_cond, occupancy, gmap):
    table, turned = plane_tables()
    vmem = pl.BlockSpec(memory_space=pltpu.VMEM)
    smem = pl.BlockSpec(memory_space=pltpu.SMEM)
    anywhere = pl.BlockSpec(memory_space=pl.ANY)
    dma = pltpu.SemaphoreType.DMA
    return pl.pallas_call(
        kernel,
        out_shape=jax.ShapeDtypeStruct((2, ROWS, WIDTH), F32),
        in_specs=[anywhere, anywhere, vmem, smem, smem, smem, anywhere, vmem, vmem],
        out_specs=vmem,
        scratch_shapes=[
            pltpu.VMEM((2, 4, DEPTH, 5184), BF16),
            pltpu.VMEM((2, 2, DEPTH, 5184), BF16),
            pltpu.VMEM((2, CHUNK, 512), BF16),
            pltpu.VMEM((8, NG), jnp.int32),
            pltpu.VMEM((CHUNKS * PLANES, CHUNK), BF16),
            pltpu.VMEM((CHUNKS * PLANES, CHUNK), BF16),
            pltpu.VMEM((352, 256), BF16),
            pltpu.VMEM((288, 256), BF16),
            pltpu.VMEM((4, 2, 16, WIDTH), F32),
            pltpu.VMEM((4, 16, WIDTH), F32),
            pltpu.VMEM((3, 16, WIDTH), F32),
            pltpu.VMEM((3, 16, WIDTH), F32),
            pltpu.VMEM((4, 16, 16, WIDTH), BF16),
            pltpu.VMEM((4, ROWS, 256), BF16),
            dma((3,)), dma((4,)), dma((4,)), dma((3,)), dma((3,)),
            dma((8,)), dma((8,)), dma((4,)), dma((4,)), dma((4, 8)), dma((4,)),
        ],
        compiler_params=pltpu.CompilerParams(
            collective_id=0, has_side_effects=True, vmem_limit_bytes=48 * 1024 * 1024
        ),
        cost_estimate=pl.CostEstimate(flops=8_000_000_000, bytes_accessed=6_000_000, transcendentals=0),
    )(
        psi_val, psi_cond, gmap, energy_val, energy_cond, occupancy,
        jnp.asarray(table), jnp.asarray(turned), jnp.asarray(depth_tables()),
    )


def solution(mesh):
    return jax.shard_map(
        shards,
        mesh=mesh,
        in_specs=(
            P(None, "val", "gcol", None),
            P(None, "cond", "gcol", None),
            P("val"),
            P("cond"),
            P("val"),
            P(),
        ),
        out_specs=P(None, ("val", "cond"), "gcol"),
        check_vma=False,
    )
```

time: 690 us -> 59.8 us (0.09)
  the two profiles are of different devices: /device:TPU:38 before, /device:TPU:5 now
where the time goes in v1:
time: 59.8 us; the launch traced here: 59.7 us
  Pallas kernels  56.3 us (94%)
  local copies, waits for them, and re-layouts  3.26 us (5%)
    pallas_call x1, Pallas kernels, shards(): pl.pallas_call(kernel, out_shape=jax.ShapeDtypeStruct((2, ROWS, WIDTH), F...  56.3 us
    unnamed x17, local copies, waits for them, and re-layouts  3.26 us

profile of v1, /device:TPU:5, one launch (start us, length us, event | category | flops | bytes accessed | tf_op | source)
XLA Modules:
  0.0 59.7 jit_solution(10611705699376359064)
XLA Ops:
  0.0 0.0 copy-start.5
  0.0 0.0 copy-start.6
  0.0 0.0 copy-start.4
  0.0 0.0 copy-start
  0.0 0.0 copy-start.3
  0.0 0.0 copy-start.2
  0.0 0.0 copy-start.1
  0.0 1.2 %copy.11.cond_hbm = bf16[2,2,9,5184]{3,2,1,0:T(8,128)(2,1)S(1)} copy(bf16[2,2,9,5184]{3,1,2,0:T(2,128)(2,1)} %param.10) | data formatting | bytes 746496 | tf_op args[1]
  1.3 1.3 %copy.10.val_hbm = bf16[2,4,9,5184]{3,2,1,0:T(8,128)(2,1)S(1)} copy(bf16[2,4,9,5184]{3,1,2,0:T(4,128)(2,1)} %param.9) | data formatting | bytes 1492992 | tf_op args[0]
  2.5 0.0 copy-done.5
  2.5 0.0 copy-done.6
  2.5 0.0 copy-done.4
  2.6 0.0 copy-done
  2.6 0.0 copy-done.3
  2.6 0.0 copy-done.2
  2.6 0.0 copy-done.1
  2.6 56.3 %shard_map.91 = f32[2,80,640]{2,1,0:T(8,128)S(1)} custom-call(bf16[2,4,9,5184]{3,2,1,0:T(8,128)(2,1)S(1)} %copy.10.val_hbm, bf16[2,2,9,5184]{3,2,1,0:T(8,128)(2,1)S(1)} %copy.11.cond_hbm, s32[3,5120]{1,0:T(4,128)S(1)} %copy-done, f32[4]{0:T(128)S(1)} %copy-done.1, f32[2]{0:T(128)S(1)} %copy-done.2, s32[4]{0:T(128)S(1)} %copy-done.3, ...), custom_call_target="tpu_custom_call" | custom-call | flops 8000000000 | bytes 6000000 | tf_op jit(solution)/shard_map/pallas_call | solution.py:335
  58.9 0.8 %copy.13 = f32[2,80,640]{2,1,0:T(8,128)} copy(f32[2,80,640]{2,1,0:T(8,128)S(1)} %shard_map.91) | data formatting | bytes 819200
Async XLA Ops:
  0.0 2.5 %copy-start.5 = (bf16[8,64,256]{2,1,0:T(8,128)(2,1)S(1)}, bf16[8,64,256]{2,1,0:T(8,128)(2,1)}, u32[]{:S(2)}) copy-start(bf16[8,64,256]{2,1,0:T(8,128)(2,1)} %constant.8.clone.depth_ref) | copy-start | bytes 786436
  0.0 2.5 %copy-start.6 = (f32[16,256]{1,0:T(8,128)S(1)}, f32[16,256]{1,0:T(8,128)}, u32[]{:S(2)}) copy-start(f32[16,256]{1,0:T(8,128)} %constant.7.clone.turn_ref) | copy-start | bytes 49156
  0.0 2.5 %copy-start.4 = (bf16[2,1152,512]{2,1,0:T(8,128)(2,1)S(1)}, bf16[2,1152,512]{2,1,0:T(8,128)(2,1)}, u32[]{:S(2)}) copy-start(bf16[2,1152,512]{2,1,0:T(8,128)(2,1)} %constant.6.clone.table_hbm) | copy-start | bytes 7077892
  0.0 2.6 %copy-start = (s32[3,5120]{1,0:T(4,128)S(1)}, s32[3,5120]{1,0:T(4,128)}, u32[]{:S(2)}) copy-start(s32[3,5120]{1,0:T(4,128)} %gmap_ref.1) | copy-start | bytes 184324
  0.0 2.6 %copy-start.3 = (s32[4]{0:T(128)S(1)}, s32[4]{0:T(128)}, u32[]{:S(2)}) copy-start(s32[4]{0:T(128)} %occ_ref.1) | copy-start | bytes 52
  0.0 2.6 %copy-start.2 = (f32[2]{0:T(128)S(1)}, f32[2]{0:T(128)}, u32[]{:S(2)}) copy-start(f32[2]{0:T(128)} %ec_ref.1) | copy-start | bytes 28
  0.0 2.6 %copy-start.1 = (f32[4]{0:T(128)S(1)}, f32[4]{0:T(128)}, u32[]{:S(2)}) copy-start(f32[4]{0:T(128)} %ev_ref.1) | copy-start | bytes 52

commit v2 on v1

--- a/solution.py
+++ b/solution.py
@@ -67,11 +67,11 @@
 
 
 def kernel(
-    val_hbm, cond_hbm, gmap_ref, ev_ref, ec_ref, occ_ref, table_hbm, turn_ref, depth_ref,
+    val_hbm, cond_hbm, gmap_hbm, ev_hbm, ec_hbm, occ_hbm, table_hbm, turn_hbm, depth_hbm,
     out_ref,
-    val_ref, cond_ref, table_ref, index_ref, high_ref, low_ref, left_ref, right_ref,
+    val_ref, cond_ref, gmap_ref, ev_ref, ec_ref, occ_ref, table_ref, turn_ref, depth_ref, index_ref, high_ref, low_ref, left_ref, right_ref,
     part, sib, xout, xin, gathered, row_buf,
-    in_sem, sib_s, sib_r, xs, xr, zs, zr, ys, yr, rs, rr,
+    in_sem, sib_s, sib_r, xs, xr, fs, fr, zs, zr, ys, yr, rs, rr,
 ):
     z_lo = lax.axis_index("val")
     cond = lax.axis_index("cond")
@@ -108,12 +108,18 @@
         pl.semaphore_signal(barrier, inc=1, device_id=peer, device_id_type=MESH)
 
     loads = [
-        pltpu.make_async_copy(val_hbm, val_ref, in_sem.at[0]),
-        pltpu.make_async_copy(cond_hbm, cond_ref, in_sem.at[1]),
-        pltpu.make_async_copy(table_hbm, table_ref, in_sem.at[2]),
+        pltpu.make_async_copy(src, dst, in_sem.at[n])
+        for n, (src, dst) in enumerate(
+            [
+                (gmap_hbm, gmap_ref), (val_hbm, val_ref), (cond_hbm, cond_ref), (table_hbm, table_ref),
+                (turn_hbm, turn_ref), (depth_hbm.at[gcol], depth_ref),
+                (ev_hbm, ev_ref), (ec_hbm, ec_ref), (occ_hbm, occ_ref),
+            ]
+        )
     ]
     for load in loads:
         load.start()
+    loads[0].wait()
 
     freq = gmap_ref[...]
     freq = jnp.where(freq > LENGTH // 2, freq - LENGTH, freq)
@@ -125,33 +131,24 @@
     pad = (CHUNKS - 1) * PLANES
     high_ref[pad:, 576:] = jnp.zeros((PLANES, CHUNK - 576), BF16)
     low_ref[pad:, 576:] = jnp.zeros((PLANES, CHUNK - 576), BF16)
-    loads[0].wait()
     loads[1].wait()
+    loads[2].wait()
 
     for chunk in range(CHUNKS):
         for begin, width in ((0, 384), (384, 384), (768, 384)) if chunk < 4 else ((0, 384), (384, 192)):
             span = pl.ds(chunk * CHUNK + begin, width)
-            v = [[val_ref[c, b, :, span].astype(F32) for b in range(4)] for c in range(2)]
-            w = [[cond_ref[c, b, :, span].astype(F32) for b in range(2)] for c in range(2)]
             sub = lax.broadcasted_iota(jnp.int32, (8, width), 0)
-
-            def last(rows, count):
-                spread = [jnp.broadcast_to(r[8:9], (8, width)) for r in rows]
-                if count == 2:
-                    return jnp.where(sub % 2 == 0, spread[0], spread[1])
-                lower = jnp.where(sub < 2, spread[0], spread[1])
-                upper = jnp.where(sub < 6, spread[2], spread[3])
-                return jnp.where(sub < 4, lower, upper)
-
             real, imag = [], []
-            for b in range(4):
-                for d in range(2):
-                    vr, vi, wr, wi = v[0][b][0:8], v[1][b][0:8], w[0][d][0:8], w[1][d][0:8]
-                    real.append(vr * wr + vi * wi)
-                    imag.append(vr * wi - vi * wr)
-            vr, vi, wr, wi = last(v[0], 4), last(v[1], 4), last(w[0], 2), last(w[1], 2)
-            real.append(vr * wr + vi * wi)
-            imag.append(vr * wi - vi * wr)
+            for d in range(DEPTH):
+                v, w = [], []
+                for c in range(2):
+                    four = val_ref[c, d, :, span].astype(F32)
+                    v.append(jnp.concatenate([four, four], axis=0))
+                    two = cond_ref[c, d, :, span].astype(F32)
+                    spread = [jnp.broadcast_to(two[i : i + 1], (8, width)) for i in range(2)]
+                    w.append(jnp.where(sub < 4, spread[0], spread[1]))
+                real.append(v[0] * w[0] + v[1] * w[1])
+                imag.append(v[0] * w[1] - v[1] * w[0])
             field = jnp.concatenate(real + imag, axis=0)
             high = field.astype(BF16)
             low = (field - high.astype(F32)).astype(BF16)
@@ -159,7 +156,8 @@
             high_ref[rows, begin : begin + width] = high
             low_ref[rows, begin : begin + width] = low
 
-    loads[2].wait()
+    for load in loads[3:]:
+        load.wait()
     planes = dot(high_ref[...], table_ref[0]) + dot(low_ref[...], table_ref[0]) + dot(high_ref[...], table_ref[1])
     cos_sum = planes[0:PLANES, 0:256]
     sin_sum = planes[0:PLANES, 256:512]
@@ -170,16 +168,12 @@
         cos_sum += c_turn * c_part - s_turn * s_part
         sin_sum += s_turn * c_part + c_turn * s_part
 
-    def by_plane(rows):
-        first = jnp.swapaxes(rows[0:64].reshape(8, 8, 256), 0, 1).reshape(64, 256)
-        return jnp.concatenate([first, rows[64:72]], axis=0)
-
-    even = jnp.concatenate([by_plane(cos_sum[0:72]), by_plane(cos_sum[72:144])], axis=0)
-    odd = jnp.concatenate([by_plane(sin_sum[72:144]), -by_plane(sin_sum[0:72])], axis=0)
+    even = cos_sum
+    odd = jnp.concatenate([sin_sum[72:144], -sin_sum[0:72]], axis=0)
     even_high, odd_high = even.astype(BF16), odd.astype(BF16)
     left_ref[0:144, :] = even_high
     left_ref[144:288, :] = (even - even_high.astype(F32)).astype(BF16)
-    left_ref[288:352, :] = depth_ref[gcol]
+    left_ref[288:352, :] = depth_ref[...]
     right_ref[0:144, :] = odd_high
     right_ref[144:288, :] = (odd - odd_high.astype(F32)).astype(BF16)
 
@@ -228,10 +222,10 @@
     e_cond = jnp.zeros((16, 1), F32)
     occupied = jnp.zeros((16, 1), F32)
     for b in range(4):
-        e_val = jnp.where(pair // 2 == b, ev_ref[b], e_val)
-        occupied = jnp.where(pair // 2 == b, occ_ref[b].astype(F32), occupied)
+        e_val = jnp.where(pair % 4 == b, ev_ref[b], e_val)
+        occupied = jnp.where(pair % 4 == b, occ_ref[b].astype(F32), occupied)
     for d in range(2):
-        e_cond = jnp.where(pair % 2 == d, ec_ref[d], e_cond)
+        e_cond = jnp.where(pair // 4 == d, ec_ref[d], e_cond)
     factor = jnp.sqrt(occupied / (e_cond - e_val) * (1.0 / math.sqrt(512.0)))
 
     sib_copies[3].wait_recv()
@@ -239,27 +233,39 @@
     for j in range(3):
         x_copies[j].wait_recv()
         total += xin[j]
-    gathered[0, 0] = (total * factor).astype(BF16)
-
-    z_copies = [
-        remote(gathered.at[0, 0], gathered.at[0, a], zs.at[a], zr.at[a], z_peer(4 * a)) for a in (2, 1, 3)
+    gathered[z_hi, 0, 0] = (total * factor).astype(BF16)
+
+    far_copies = [
+        remote(gathered.at[z_hi, 0, 0], gathered.at[z_hi, 0, 0], fs.at[a], fr.at[z_hi], z_peer(4 * a)) for a in (2, 1, 3)
     ]
-    for copy in z_copies:
+
+    def near_copies(q):
+        steps = ((1, 1), (15, 3), (2 - 4 * ((q + 1) // 2 % 2), 2))
+        return [
+            remote(gathered.at[q, 0, 0], gathered.at[q, 0, m], zs.at[q, m], zr.at[q, m], z_peer(step))
+            for step, m in steps
+        ]
+
+    def y_copies(q):
+        return [remote(gathered.at[q, 0], gathered.at[q, j], ys.at[q, j], yr.at[q, j], y_peer(j)) for j in (1, 3, 2)]
+
+    def pass_on(q):
+        @pl.when(z_hi != q)
+        def _():
+            remote(gathered.at[q, 0, 0], gathered.at[q, 0, 0], fs.at[0], fr.at[q], z_peer(4)).wait_recv()
+            for copy in near_copies(q):
+                copy.start()
+
+    def share_y(q):
+        for copy in near_copies(q):
+            copy.wait_recv()
+        for copy in y_copies(q):
+            copy.start()
+
+    for copy in far_copies:
         copy.start()
-    for copy in z_copies:
-        copy.wait_recv()
-    near = [(1, 0, 4, 4), (15, 0, 12, 4), (2, 1, 8, 2), (14, 0, 10, 2)]
-    near_copies = [
-        remote(gathered.at[0, pl.ds(src, n)], gathered.at[0, pl.ds(dst, n)], zs.at[4 + i], zr.at[4 + i], z_peer(step))
-        for i, (step, src, dst, n) in enumerate(near)
-    ]
-    for copy in near_copies:
+    for copy in near_copies(z_hi):
         copy.start()
-    for copy in near_copies:
-        copy.wait_recv()
-    y_copies = {j: remote(gathered.at[0], gathered.at[j], ys.at[j], yr.at[j], y_peer(j)) for j in (1, 3, 2)}
-    for j in (1, 3, 2):
-        y_copies[j].start()
 
     is_source = gcol == z_lo * 2 + cond // 8
     offset = cond % 8 * ROWS
@@ -280,6 +286,9 @@
         return remote(row_buf.at[j], row_buf.at[j], rs.at[j, step], rr.at[j], g_peer(step))
 
     def share_rows(j):
+        for copy in y_copies(j):
+            copy.wait_recv()
+
         @pl.when(is_source)
         def _():
             columns = gathered[j].reshape(256, WIDTH)
@@ -304,14 +313,19 @@
             out_ref[0] += real
             out_ref[1] += imag
 
+    pass_on(0)
+    pass_on(1)
+    share_y(0)
+    pass_on(3)
+    share_y(1)
     share_rows(0)
-    y_copies[1].wait_recv()
+    pass_on(2)
+    share_y(3)
     share_rows(1)
     use(0, True)
-    y_copies[3].wait_recv()
+    share_y(2)
     share_rows(3)
     use(1, False)
-    y_copies[2].wait_recv()
     share_rows(2)
     use(3, False)
     use(2, False)
@@ -322,25 +336,33 @@
             for step in range(1, 8):
                 row_copy(j, step).wait_send()
 
-    for copy in sib_copies + x_copies + z_copies + near_copies + list(y_copies.values()):
+    for copy in sib_copies + x_copies + far_copies:
         copy.wait_send()
+    for q in range(4):
+        for copy in near_copies(q) + y_copies(q):
+            copy.wait_send()
 
 
 def shards(psi_val, psi_cond, energy_val, energy_cond, occupancy, gmap):
     table, turned = plane_tables()
     vmem = pl.BlockSpec(memory_space=pltpu.VMEM)
-    smem = pl.BlockSpec(memory_space=pltpu.SMEM)
-    anywhere = pl.BlockSpec(memory_space=pl.ANY)
+    hbm = pl.BlockSpec(memory_space=pltpu.HBM)
     dma = pltpu.SemaphoreType.DMA
     return pl.pallas_call(
         kernel,
         out_shape=jax.ShapeDtypeStruct((2, ROWS, WIDTH), F32),
-        in_specs=[anywhere, anywhere, vmem, smem, smem, smem, anywhere, vmem, vmem],
+        in_specs=[hbm] * 9,
         out_specs=vmem,
         scratch_shapes=[
-            pltpu.VMEM((2, 4, DEPTH, 5184), BF16),
-            pltpu.VMEM((2, 2, DEPTH, 5184), BF16),
+            pltpu.VMEM((2, DEPTH, 4, 5184), BF16),
+            pltpu.VMEM((2, DEPTH, 2, 5184), BF16),
+            pltpu.VMEM((3, NG), jnp.int32),
+            pltpu.SMEM((4,), F32),
+            pltpu.SMEM((2,), F32),
+            pltpu.SMEM((4,), jnp.int32),
             pltpu.VMEM((2, CHUNK, 512), BF16),
+            pltpu.VMEM((16, 256), F32),
+            pltpu.VMEM((64, 256), BF16),
             pltpu.VMEM((8, NG), jnp.int32),
             pltpu.VMEM((CHUNKS * PLANES, CHUNK), BF16),
             pltpu.VMEM((CHUNKS * PLANES, CHUNK), BF16),
@@ -350,17 +372,17 @@
             pltpu.VMEM((4, 16, WIDTH), F32),
             pltpu.VMEM((3, 16, WIDTH), F32),
             pltpu.VMEM((3, 16, WIDTH), F32),
-            pltpu.VMEM((4, 16, 16, WIDTH), BF16),
+            pltpu.VMEM((4, 4, 4, 16, WIDTH), BF16),
             pltpu.VMEM((4, ROWS, 256), BF16),
-            dma((3,)), dma((4,)), dma((4,)), dma((3,)), dma((3,)),
-            dma((8,)), dma((8,)), dma((4,)), dma((4,)), dma((4, 8)), dma((4,)),
+            dma((9,)), dma((4,)), dma((4,)), dma((3,)), dma((3,)),
+            dma((4,)), dma((4,)), dma((4, 4)), dma((4, 4)), dma((4, 4)), dma((4, 4)), dma((4, 8)), dma((4,)),
         ],
         compiler_params=pltpu.CompilerParams(
-            collective_id=0, has_side_effects=True, vmem_limit_bytes=48 * 1024 * 1024
+            collective_id=0, has_side_effects=True, vmem_limit_bytes=64 * 1024 * 1024
         ),
         cost_estimate=pl.CostEstimate(flops=8_000_000_000, bytes_accessed=6_000_000, transcendentals=0),
     )(
-        psi_val, psi_cond, gmap, energy_val, energy_cond, occupancy,
+        jnp.swapaxes(psi_val, 1, 2), jnp.swapaxes(psi_cond, 1, 2), gmap, energy_val, energy_cond, occupancy,
         jnp.asarray(table), jnp.asarray(turned), jnp.asarray(depth_tables()),
     )
 

time: 59.8 us -> 57.5 us (0.962)
  local copies, waits for them, and re-layouts: 3.26 us -> 1.78 us
  Pallas kernels: 56.3 us -> 55.6 us
    unnamed x17 -> x1, local copies, waits for them, and re-layouts: 3.26 us -> 1.78 us
    pallas_call x1, Pallas kernels: 56.3 us -> 55.6 us  [shards(): pl.pallas_call(kernel, out_shape=jax.ShapeDtypeStruct((2, ROWS, WIDTH), F...]
where the time goes in v2:
time: 57.5 us; the launch traced here: 57.4 us
  Pallas kernels  55.6 us (97%)
  local copies, waits for them, and re-layouts  1.78 us (3%)
    pallas_call x1, Pallas kernels, shards(): pl.pallas_call(kernel, out_shape=jax.ShapeDtypeStruct((2, ROWS, WIDTH), F...  55.6 us
    unnamed x1, local copies, waits for them, and re-layouts  1.78 us

profile of v2, /device:TPU:5, one launch (start us, length us, event | category | flops | bytes accessed | tf_op | source)
XLA Modules:
  0.0 57.4 jit_solution(8112657203159656620)
XLA Ops:
  0.0 55.6 %shard_map.91 = f32[2,80,640]{2,1,0:T(8,128)} custom-call(bf16[2,9,4,5184]{3,2,1,0:T(4,128)(2,1)} %bitcast.2, bf16[2,9,2,5184]{3,2,1,0:T(2,128)(2,1)} %bitcast.3, s32[3,5120]{1,0:T(4,128)} %gmap_hbm.1, f32[4]{0:T(128)} %ev_hbm.1, f32[2]{0:T(128)} %ec_hbm.1, s32[4]{0:T(128)} %occ_hbm.1, bf16[2,1152,512]{2,1,0:T(8,128)(2,1)} %constant.6.clone.table_hbm, ...), custom_call_target="tpu_custom_call" | custom-call | flops 8000000000 | bytes 6000000 | tf_op jit(solution)/shard_map/pallas_call | solution.py:351
  55.6 1.8 %copy.11 = f32[2,80,640]{2,1,0:T(8,128)} copy(f32[2,80,640]{2,1,0:T(8,128)} %shard_map.91) | data formatting | bytes 819200

commit v3 on v2

--- a/solution.py
+++ b/solution.py
@@ -20,6 +20,7 @@
 DEPTH = 9
 WIDTH = 640
 ROWS = 80
+MAIN = 384
 PLANES = 144
 F32 = jnp.float32
 BF16 = jnp.bfloat16
@@ -70,8 +71,8 @@
     val_hbm, cond_hbm, gmap_hbm, ev_hbm, ec_hbm, occ_hbm, table_hbm, turn_hbm, depth_hbm,
     out_ref,
     val_ref, cond_ref, gmap_ref, ev_ref, ec_ref, occ_ref, table_ref, turn_ref, depth_ref, index_ref, high_ref, low_ref, left_ref, right_ref,
-    part, sib, xout, xin, gathered, row_buf,
-    in_sem, sib_s, sib_r, xs, xr, fs, fr, zs, zr, ys, yr, rs, rr,
+    part, sib, xout, xin, gathered, row_buf, row_out, row_in,
+    in_sem, sib_s, sib_r, xs, xr, fs, fr, zs, zr, ys, yr, rs, rr, ps, pr, vs, vr, us, ur,
 ):
     z_lo = lax.axis_index("val")
     cond = lax.axis_index("cond")
@@ -106,6 +107,18 @@
     barrier = pltpu.get_barrier_semaphore()
     for peer in peers:
         pl.semaphore_signal(barrier, inc=1, device_id=peer, device_id_type=MESH)
+    is_source = gcol == z_lo * 2 + cond // 8
+
+    @pl.when(is_source)
+    def _():
+        @pl.loop(0, 64)
+        def _(n):
+            @pl.when(n != y * 16 + z)
+            def _():
+                pl.semaphore_signal(
+                    barrier, inc=1, device_id=device(x, n // 16, n % 16, core), device_id_type=MESH
+                )
+
 
     loads = [
         pltpu.make_async_copy(src, dst, in_sem.at[n])
@@ -177,16 +190,17 @@
     right_ref[0:144, :] = odd_high
     right_ref[144:288, :] = (odd - odd_high.astype(F32)).astype(BF16)
 
-    place = lax.broadcasted_iota(jnp.int32, (256, 256), 0)
+    place = lax.broadcasted_iota(jnp.int32, (256, 256), 0).astype(F32).astype(BF16)
+    one, nil = jnp.ones((256, 256), BF16), jnp.zeros((256, 256), BF16)
 
     def block(step):
         target = (x + 3 - step) % 4
         for piece in range(5):
             span = pl.ds(pl.multiple_of(target * 1280 + piece * 256, 256), 256)
-            hit = place == index_ref[0:1, span]
-            phase = place == index_ref[2:3, span]
-            pick = jnp.where(hit | phase, 1.0, 0.0).astype(BF16)
-            signed = jnp.where(hit, index_ref[1:2, span].astype(F32), 0.0).astype(BF16)
+            hit = place == index_ref[0:1, span].astype(F32).astype(BF16)
+            phase = place == index_ref[2:3, span].astype(F32).astype(BF16)
+            pick = jnp.where(hit | phase, one, nil)
+            signed = jnp.where(hit, jnp.broadcast_to(index_ref[1:2, span].astype(F32).astype(BF16), (256, 256)), nil)
             first = dot(left_ref[...], pick)
             second = dot(right_ref[...], signed)
             values = first[0:144] + first[144:288] + second[0:144] + second[144:288]
@@ -210,7 +224,7 @@
     for j in range(4):
         block(j)
         if j == 0:
-            pl.semaphore_wait(barrier, len(peers))
+            pl.semaphore_wait(barrier, len(peers) + 8 - is_source.astype(jnp.int32))
         sib_copies[j].start()
         if j > 0:
             sib_copies[j - 1].wait_recv()
@@ -233,47 +247,79 @@
     for j in range(3):
         x_copies[j].wait_recv()
         total += xin[j]
-    gathered[z_hi, 0, 0] = (total * factor).astype(BF16)
-
+    scaled = total * factor
+    gathered[z_hi, 0, 0] = scaled.astype(BF16)
+
+    main, rest = pl.ds(0, MAIN), pl.ds(MAIN, WIDTH - MAIN)
     far_copies = [
         remote(gathered.at[z_hi, 0, 0], gathered.at[z_hi, 0, 0], fs.at[a], fr.at[z_hi], z_peer(4 * a)) for a in (2, 1, 3)
     ]
 
-    def near_copies(q):
-        steps = ((1, 1), (15, 3), (2 - 4 * ((q + 1) // 2 % 2), 2))
+    def near_steps(q):
+        return ((1, 1), (15, 3), (2 - 4 * ((q + 1) // 2 % 2), 2))
+
+    def near_main(q):
+        own = gathered.at[q, 0, 0, :, main]
         return [
-            remote(gathered.at[q, 0, 0], gathered.at[q, 0, m], zs.at[q, m], zr.at[q, m], z_peer(step))
-            for step, m in steps
+            remote(own, gathered.at[q, 0, m, :, main], zs.at[q, m], zr.at[q, m], z_peer(step))
+            for step, m in near_steps(q)
         ]
 
-    def y_copies(q):
-        return [remote(gathered.at[q, 0], gathered.at[q, j], ys.at[q, j], yr.at[q, j], y_peer(j)) for j in (1, 3, 2)]
+    def y_main(q):
+        own = gathered.at[q, 0, :, :, main]
+        return [remote(own, gathered.at[q, j, :, :, main], ys.at[q, j], yr.at[q, j], y_peer(j)) for j in (2, 1, 3)]
+
+    def y_rest(q):
+        own = gathered.at[q, 0, 0, :, rest]
+        return [remote(own, gathered.at[q, j, 0, :, rest], vs.at[q, j], vr.at[q, j], y_peer(j)) for j in (2, 1, 3)]
+
+    def near_rest(q):
+        own = gathered.at[q, :, 0, :, rest]
+        return [
+            remote(own, gathered.at[q, :, m, :, rest], us.at[q, m], ur.at[q, m], z_peer(step))
+            for step, m in near_steps(q)
+        ]
+
+    def start(copies):
+        for copy in copies:
+            copy.start()
+
+    def arrived(copies):
+        for copy in copies:
+            copy.wait_recv()
 
     def pass_on(q):
         @pl.when(z_hi != q)
         def _():
             remote(gathered.at[q, 0, 0], gathered.at[q, 0, 0], fs.at[0], fr.at[q], z_peer(4)).wait_recv()
-            for copy in near_copies(q):
-                copy.start()
-
-    def share_y(q):
-        for copy in near_copies(q):
-            copy.wait_recv()
-        for copy in y_copies(q):
-            copy.start()
-
-    for copy in far_copies:
-        copy.start()
-    for copy in near_copies(z_hi):
-        copy.start()
-
-    is_source = gcol == z_lo * 2 + cond // 8
-    offset = cond % 8 * ROWS
+            start(near_main(q) + y_rest(q))
+
+    def share_main(q):
+        arrived(near_main(q))
+        start(y_main(q))
+
+    def share_rest(q):
+        arrived(y_rest(q))
+        start(near_rest(q))
+
+    start(far_copies + near_main(z_hi) + y_rest(z_hi))
+
+    def row_piece(b):
+        y_to, z_to = 2 * core + b // 4, b % 4 * 4 + x
+        slot = row_in.at[z_hi, (y_to - y + 4) % 4, (z_to - z + 16) % 4]
+        far = remote(row_out.at[b], slot, ps.at[b], pr.at[z_hi], device(x, y_to, z_to, core))
+        near = pltpu.make_async_copy(row_out.at[b], slot, pr.at[z_hi])
+        return far, near, (y_to == y) & (z_to == z)
+
+    for b in range(8):
+        cut = scaled[:, b * ROWS : (b + 1) * ROWS]
+        row_out[b] = jnp.concatenate([cut, jnp.zeros((16, 128 - ROWS), F32)], axis=1).astype(BF16)
+        far, near, own = row_piece(b)
+        pl.when(own)(near.start)
+        pl.when(jnp.logical_not(own))(far.start)
+
     chosen = jnp.where(
-        lax.broadcasted_iota(jnp.int32, (ROWS, WIDTH), 1)
-        == lax.broadcasted_iota(jnp.int32, (ROWS, WIDTH), 0) + offset,
-        1.0,
-        0.0,
+        lax.broadcasted_iota(jnp.int32, (ROWS, 128), 1) == lax.broadcasted_iota(jnp.int32, (ROWS, 128), 0), 1.0, 0.0
     ).astype(BF16)
     k_row = lax.broadcasted_iota(jnp.int32, (256, 256), 0)
     k_col = lax.broadcasted_iota(jnp.int32, (256, 256), 1)
@@ -286,18 +332,18 @@
         return remote(row_buf.at[j], row_buf.at[j], rs.at[j, step], rr.at[j], g_peer(step))
 
     def share_rows(j):
-        for copy in y_copies(j):
-            copy.wait_recv()
-
         @pl.when(is_source)
         def _():
-            columns = gathered[j].reshape(256, WIDTH)
-            rows = lax.dot_general(chosen, columns, (((1,), (1,)), ((), ())), preferred_element_type=F32)
+            pltpu.make_async_copy(row_in.at[j], row_in.at[j], pr.at[j]).wait()
+            pieces = row_in[j].reshape(256, 128)
+            rows = lax.dot_general(chosen, pieces, (((1,), (1,)), ((), ())), preferred_element_type=F32)
             row_buf[j] = rows.astype(BF16)
             for step in range(1, 8):
                 row_copy(j, step).start()
 
     def use(j, first):
+        arrived(y_main(j) + near_rest(j))
+
         @pl.when(jnp.logical_not(is_source))
         def _():
             row_copy(j, 1).wait_recv()
@@ -315,20 +361,28 @@
 
     pass_on(0)
     pass_on(1)
-    share_y(0)
     pass_on(3)
-    share_y(1)
+    pass_on(2)
+    share_main(0)
+    share_rest(0)
+    share_main(1)
+    share_rest(1)
     share_rows(0)
-    pass_on(2)
-    share_y(3)
+    share_main(3)
+    share_rest(3)
     share_rows(1)
+    share_main(2)
+    share_rest(2)
+    share_rows(3)
+    share_rows(2)
     use(0, True)
-    share_y(2)
-    share_rows(3)
     use(1, False)
-    share_rows(2)
     use(3, False)
     use(2, False)
+
+    for b in range(8):
+        far, _, own = row_piece(b)
+        pl.when(jnp.logical_not(own))(far.wait_send)
 
     @pl.when(is_source)
     def _():
@@ -339,7 +393,7 @@
     for copy in sib_copies + x_copies + far_copies:
         copy.wait_send()
     for q in range(4):
-        for copy in near_copies(q) + y_copies(q):
+        for copy in near_main(q) + y_main(q) + y_rest(q) + near_rest(q):
             copy.wait_send()
 
 
@@ -374,8 +428,11 @@
             pltpu.VMEM((3, 16, WIDTH), F32),
             pltpu.VMEM((4, 4, 4, 16, WIDTH), BF16),
             pltpu.VMEM((4, ROWS, 256), BF16),
+            pltpu.VMEM((8, 16, 128), BF16),
+            pltpu.VMEM((4, 4, 4, 16, 128), BF16),
             dma((9,)), dma((4,)), dma((4,)), dma((3,)), dma((3,)),
-            dma((4,)), dma((4,)), dma((4, 4)), dma((4, 4)), dma((4, 4)), dma((4, 4)), dma((4, 8)), dma((4,)),
+            dma((4,)), dma((4,)), dma((4, 4)), dma((4, 4)), dma((4, 4)), dma((4, 4)), dma((4, 8)), dma((4,)), dma((8,)), dma((4,)),
+            dma((4, 4)), dma((4, 4)), dma((4, 4)), dma((4, 4)),
         ],
         compiler_params=pltpu.CompilerParams(
             collective_id=0, has_side_effects=True, vmem_limit_bytes=64 * 1024 * 1024

time: 57.5 us -> 50.2 us (0.87)
  the two profiles are of different devices: /device:TPU:5 before, /device:TPU:2 now
where the time goes in v3:
time: 50.2 us; the launch traced here: 50 us
  Pallas kernels  48.2 us (96%)
  local copies, waits for them, and re-layouts  1.78 us (4%)
    pallas_call x1, Pallas kernels, shards(): pl.pallas_call(kernel, out_shape=jax.ShapeDtypeStruct((2, ROWS, WIDTH), F...  48.2 us
    unnamed x1, local copies, waits for them, and re-layouts  1.78 us

profile of v3, /device:TPU:2, one launch (start us, length us, event | category | flops | bytes accessed | tf_op | source)
XLA Modules:
  0.0 50.0 jit_solution(15641811309746833723)
XLA Ops:
  0.0 48.2 %shard_map.91 = f32[2,80,640]{2,1,0:T(8,128)} custom-call(bf16[2,9,4,5184]{3,2,1,0:T(4,128)(2,1)} %bitcast.2, bf16[2,9,2,5184]{3,2,1,0:T(2,128)(2,1)} %bitcast.3, s32[3,5120]{1,0:T(4,128)} %gmap_hbm.1, f32[4]{0:T(128)} %ev_hbm.1, f32[2]{0:T(128)} %ec_hbm.1, s32[4]{0:T(128)} %occ_hbm.1, bf16[2,1152,512]{2,1,0:T(8,128)(2,1)} %constant.6.clone.table_hbm, ...), custom_call_target="tpu_custom_call" | custom-call | flops 8000000000 | bytes 6000000 | tf_op jit(solution)/shard_map/pallas_call | solution.py:405
  48.3 1.8 %copy.11 = f32[2,80,640]{2,1,0:T(8,128)} copy(f32[2,80,640]{2,1,0:T(8,128)} %shard_map.91) | data formatting | bytes 819200

commit v4 on v3

--- a/solution.py
+++ b/solution.py
@@ -104,27 +104,11 @@
     peers = [g_peer(s) for s in range(1, 8)]
     peers += [z_peer(s) for s in (1, 2, 4, 8, 12, 14, 15)]
     peers += [y_peer(s) for s in (1, 2, 3)]
-    barrier = pltpu.get_barrier_semaphore()
-    for peer in peers:
-        pl.semaphore_signal(barrier, inc=1, device_id=peer, device_id_type=MESH)
-    is_source = gcol == z_lo * 2 + cond // 8
-
-    @pl.when(is_source)
-    def _():
-        @pl.loop(0, 64)
-        def _(n):
-            @pl.when(n != y * 16 + z)
-            def _():
-                pl.semaphore_signal(
-                    barrier, inc=1, device_id=device(x, n // 16, n % 16, core), device_id_type=MESH
-                )
-
-
     loads = [
         pltpu.make_async_copy(src, dst, in_sem.at[n])
         for n, (src, dst) in enumerate(
             [
-                (gmap_hbm, gmap_ref), (val_hbm, val_ref), (cond_hbm, cond_ref), (table_hbm, table_ref),
+                (gmap_hbm, gmap_ref), (val_hbm, val_ref), (cond_hbm, cond_ref), (table_hbm.at[0], table_ref.at[0]), (table_hbm.at[1], table_ref.at[1]),
                 (turn_hbm, turn_ref), (depth_hbm.at[gcol], depth_ref),
                 (ev_hbm, ev_ref), (ec_hbm, ec_ref), (occ_hbm, occ_ref),
             ]
@@ -132,6 +116,21 @@
     ]
     for load in loads:
         load.start()
+    barrier = pltpu.get_barrier_semaphore()
+    for peer in peers:
+        pl.semaphore_signal(barrier, inc=1, device_id=peer, device_id_type=MESH)
+    is_source = gcol == z_lo * 2 + cond // 8
+
+    @pl.when(is_source)
+    def _():
+        for n in range(64):
+
+            @pl.when(n != y * 16 + z)
+            def _(n=n):
+                pl.semaphore_signal(
+                    barrier, inc=1, device_id=device(x, n // 16, n % 16, core), device_id_type=MESH
+                )
+
     loads[0].wait()
 
     freq = gmap_ref[...]
@@ -169,14 +168,28 @@
             high_ref[rows, begin : begin + width] = high
             low_ref[rows, begin : begin + width] = low
 
-    for load in loads[3:]:
+    loads[3].wait()
+    full = (CHUNKS - 1) * PLANES
+
+    def transform(rows, depth):
+        return dot(high_ref[rows, 0:depth], table_ref[0, 0:depth]) + dot(low_ref[rows, 0:depth], table_ref[0, 0:depth])
+
+    def correction(rows, depth):
+        return dot(high_ref[rows, 0:depth], table_ref[1, 0:depth])
+
+    whole, half = slice(0, full), slice(full, full + PLANES)
+    planes = transform(whole, CHUNK)
+    tail = transform(half, 640)
+    for load in loads[4:]:
         load.wait()
-    planes = dot(high_ref[...], table_ref[0]) + dot(low_ref[...], table_ref[0]) + dot(high_ref[...], table_ref[1])
+    planes += correction(whole, CHUNK)
+    tail += correction(half, 640)
     cos_sum = planes[0:PLANES, 0:256]
     sin_sum = planes[0:PLANES, 256:512]
     for chunk in range(1, CHUNKS):
         at = chunk * PLANES
-        c_part, s_part = planes[at : at + PLANES, 0:256], planes[at : at + PLANES, 256:512]
+        held = planes[at : at + PLANES] if chunk < CHUNKS - 1 else tail
+        c_part, s_part = held[:, 0:256], held[:, 256:512]
         c_turn, s_turn = turn_ref[2 * chunk : 2 * chunk + 1, :], turn_ref[2 * chunk + 1 : 2 * chunk + 2, :]
         cos_sum += c_turn * c_part - s_turn * s_part
         sin_sum += s_turn * c_part + c_turn * s_part
@@ -265,19 +278,22 @@
             for step, m in near_steps(q)
         ]
 
-    def y_main(q):
-        own = gathered.at[q, 0, :, :, main]
-        return [remote(own, gathered.at[q, j, :, :, main], ys.at[q, j], yr.at[q, j], y_peer(j)) for j in (2, 1, 3)]
+    def y_main(g):
+        own = gathered.at[pl.ds(2 * g, 2), 0, :, :, main]
+        return [
+            remote(own, gathered.at[pl.ds(2 * g, 2), j, :, :, main], ys.at[g, j], yr.at[g, j], y_peer(j))
+            for j in (2, 1, 3)
+        ]
 
     def y_rest(q):
         own = gathered.at[q, 0, 0, :, rest]
         return [remote(own, gathered.at[q, j, 0, :, rest], vs.at[q, j], vr.at[q, j], y_peer(j)) for j in (2, 1, 3)]
 
-    def near_rest(q):
-        own = gathered.at[q, :, 0, :, rest]
+    def near_rest(g):
+        own = gathered.at[pl.ds(2 * g, 2), :, 0, :, rest]
         return [
-            remote(own, gathered.at[q, :, m, :, rest], us.at[q, m], ur.at[q, m], z_peer(step))
-            for step, m in near_steps(q)
+            remote(own, gathered.at[pl.ds(2 * g, 2), :, m, :, rest], us.at[g, m], ur.at[g, m], z_peer(step))
+            for step, m in near_steps(g)
         ]
 
     def start(copies):
@@ -294,13 +310,13 @@
             remote(gathered.at[q, 0, 0], gathered.at[q, 0, 0], fs.at[0], fr.at[q], z_peer(4)).wait_recv()
             start(near_main(q) + y_rest(q))
 
-    def share_main(q):
-        arrived(near_main(q))
-        start(y_main(q))
-
-    def share_rest(q):
-        arrived(y_rest(q))
-        start(near_rest(q))
+    def share_main(g):
+        arrived(near_main(2 * g) + near_main(2 * g + 1))
+        start(y_main(g))
+
+    def share_rest(g):
+        arrived(y_rest(2 * g) + y_rest(2 * g + 1))
+        start(near_rest(g))
 
     start(far_copies + near_main(z_hi) + y_rest(z_hi))
 
@@ -328,26 +344,29 @@
         is_real & (k_row == k_col + 8), 1.0, jnp.where(~is_real & (k_row == k_col - 8), -1.0, 0.0)
     ).astype(BF16)
 
-    def row_copy(j, step):
-        return remote(row_buf.at[j], row_buf.at[j], rs.at[j, step], rr.at[j], g_peer(step))
-
-    def share_rows(j):
+    def row_copy(g, step):
+        held = row_buf.at[pl.ds(2 * g, 2)]
+        return remote(held, held, rs.at[g, step], rr.at[g], g_peer(step))
+
+    def share_rows(g):
         @pl.when(is_source)
         def _():
-            pltpu.make_async_copy(row_in.at[j], row_in.at[j], pr.at[j]).wait()
-            pieces = row_in[j].reshape(256, 128)
-            rows = lax.dot_general(chosen, pieces, (((1,), (1,)), ((), ())), preferred_element_type=F32)
-            row_buf[j] = rows.astype(BF16)
+            for j in (2 * g, 2 * g + 1):
+                pltpu.make_async_copy(row_in.at[j], row_in.at[j], pr.at[j]).wait()
+                pieces = row_in[j].reshape(256, 128)
+                rows = lax.dot_general(chosen, pieces, (((1,), (1,)), ((), ())), preferred_element_type=F32)
+                row_buf[j] = rows.astype(BF16)
             for step in range(1, 8):
-                row_copy(j, step).start()
-
-    def use(j, first):
-        arrived(y_main(j) + near_rest(j))
+                row_copy(g, step).start()
+
+    def ready(g):
+        arrived(y_main(g) + near_rest(g))
 
         @pl.when(jnp.logical_not(is_source))
         def _():
-            row_copy(j, 1).wait_recv()
-
+            row_copy(g, 1).wait_recv()
+
+    def use(j, first):
         rows = row_buf[j]
         rows_i = dot(rows, turn_i).astype(BF16)
         columns = gathered[j].reshape(256, WIDTH)
@@ -363,20 +382,16 @@
     pass_on(1)
     pass_on(3)
     pass_on(2)
+    share_rows(0)
     share_main(0)
     share_rest(0)
+    share_rows(1)
     share_main(1)
     share_rest(1)
-    share_rows(0)
-    share_main(3)
-    share_rest(3)
-    share_rows(1)
-    share_main(2)
-    share_rest(2)
-    share_rows(3)
-    share_rows(2)
+    ready(0)
     use(0, True)
     use(1, False)
+    ready(1)
     use(3, False)
     use(2, False)
 
@@ -386,14 +401,17 @@
 
     @pl.when(is_source)
     def _():
-        for j in range(4):
+        for g in range(2):
             for step in range(1, 8):
-                row_copy(j, step).wait_send()
+                row_copy(g, step).wait_send()
 
     for copy in sib_copies + x_copies + far_copies:
         copy.wait_send()
     for q in range(4):
-        for copy in near_main(q) + y_main(q) + y_rest(q) + near_rest(q):
+        for copy in near_main(q) + y_rest(q):
+            copy.wait_send()
+    for g in range(2):
+        for copy in y_main(g) + near_rest(g):
             copy.wait_send()
 
 
@@ -430,7 +448,7 @@
             pltpu.VMEM((4, ROWS, 256), BF16),
             pltpu.VMEM((8, 16, 128), BF16),
             pltpu.VMEM((4, 4, 4, 16, 128), BF16),
-            dma((9,)), dma((4,)), dma((4,)), dma((3,)), dma((3,)),
+            dma((10,)), dma((4,)), dma((4,)), dma((3,)), dma((3,)),
             dma((4,)), dma((4,)), dma((4, 4)), dma((4, 4)), dma((4, 4)), dma((4, 4)), dma((4, 8)), dma((4,)), dma((8,)), dma((4,)),
             dma((4, 4)), dma((4, 4)), dma((4, 4)), dma((4, 4)),
         ],

time: 50.2 us -> 49.8 us (level)
  the two profiles are of different devices: /device:TPU:2 before, /device:TPU:1 now
where the time goes in v4:
time: 49.8 us; the launch traced here: 49.7 us
  Pallas kernels  47.9 us (96%)
  local copies, waits for them, and re-layouts  1.78 us (4%)
    pallas_call x1, Pallas kernels, shards(): pl.pallas_call(kernel, out_shape=jax.ShapeDtypeStruct((2, ROWS, WIDTH), F...  47.9 us
    unnamed x1, local copies, waits for them, and re-layouts  1.78 us

profile of v4, /device:TPU:1, one launch (start us, length us, event | category | flops | bytes accessed | tf_op | source)
XLA Modules:
  0.0 49.7 jit_solution(1744181205277764076)
XLA Ops:
  0.0 47.9 %shard_map.91 = f32[2,80,640]{2,1,0:T(8,128)} custom-call(bf16[2,9,4,5184]{3,2,1,0:T(4,128)(2,1)} %bitcast.2, bf16[2,9,2,5184]{3,2,1,0:T(2,128)(2,1)} %bitcast.3, s32[3,5120]{1,0:T(4,128)} %gmap_hbm.1, f32[4]{0:T(128)} %ev_hbm.1, f32[2]{0:T(128)} %ec_hbm.1, s32[4]{0:T(128)} %occ_hbm.1, bf16[2,1152,512]{2,1,0:T(8,128)(2,1)} %constant.6.clone.table_hbm, ...), custom_call_target="tpu_custom_call" | custom-call | flops 8000000000 | bytes 6000000 | tf_op jit(solution)/shard_map/pallas_call | solution.py:423
  47.9 1.8 %copy.11 = f32[2,80,640]{2,1,0:T(8,128)} copy(f32[2,80,640]{2,1,0:T(8,128)} %shard_map.91) | data formatting | bytes 819200

commit v5 on v4

--- a/solution.py
+++ b/solution.py
@@ -366,10 +366,11 @@
         def _():
             row_copy(g, 1).wait_recv()
 
-    def use(j, first):
-        rows = row_buf[j]
-        rows_i = dot(rows, turn_i).astype(BF16)
-        columns = gathered[j].reshape(256, WIDTH)
+    def use(g, first):
+        rows = [row_buf[2 * g], row_buf[2 * g + 1]]
+        rows_i = jnp.concatenate([dot(r, turn_i).astype(BF16) for r in rows], axis=1)
+        rows = jnp.concatenate(rows, axis=1)
+        columns = gathered[2 * g : 2 * g + 2].reshape(512, WIDTH)
         real, imag = dot(rows, columns), dot(rows_i, columns)
         if first:
             out_ref[0] = real
@@ -390,10 +391,8 @@
     share_rest(1)
     ready(0)
     use(0, True)
+    ready(1)
     use(1, False)
-    ready(1)
-    use(3, False)
-    use(2, False)
 
     for b in range(8):
         far, _, own = row_piece(b)

time: 49.8 us -> 49.7 us (level)
  no operation moved by 1% of the time
where the time goes in v5:
time: 49.7 us; the launch traced here: 49.6 us
  Pallas kernels  47.8 us (96%)
  local copies, waits for them, and re-layouts  1.78 us (4%)
    pallas_call x1, Pallas kernels, shards(): pl.pallas_call(kernel, out_shape=jax.ShapeDtypeStruct((2, ROWS, WIDTH), F...  47.8 us
    unnamed x1, local copies, waits for them, and re-layouts  1.78 us

profile of v5, /device:TPU:1, one launch (start us, length us, event | category | flops | bytes accessed | tf_op | source)
XLA Modules:
  0.0 49.6 jit_solution(10021020095990274089)
XLA Ops:
  0.0 47.8 %shard_map.91 = f32[2,80,640]{2,1,0:T(8,128)} custom-call(bf16[2,9,4,5184]{3,2,1,0:T(4,128)(2,1)} %bitcast.2, bf16[2,9,2,5184]{3,2,1,0:T(2,128)(2,1)} %bitcast.3, s32[3,5120]{1,0:T(4,128)} %gmap_hbm.1, f32[4]{0:T(128)} %ev_hbm.1, f32[2]{0:T(128)} %ec_hbm.1, s32[4]{0:T(128)} %occ_hbm.1, bf16[2,1152,512]{2,1,0:T(8,128)(2,1)} %constant.6.clone.table_hbm, ...), custom_call_target="tpu_custom_call" | custom-call | flops 8000000000 | bytes 6000000 | tf_op jit(solution)/shard_map/pallas_call | solution.py:422
  47.8 1.8 %copy.11 = f32[2,80,640]{2,1,0:T(8,128)} copy(f32[2,80,640]{2,1,0:T(8,128)} %shard_map.91) | data formatting | bytes 819200
